TPU v7x, 32 devices: a whole 2x2x4 slice. The times are simulated.
32 devices in a mesh: tm: 16 (over z, y, x), traj: 2 (over core).
Axes of the slice: x: 2, y: 2, z: 4, core: 2. Of those that a mesh axis runs over, the one named last changes fastest.
Arguments:
- init_state: float32 [32, 256], P('traj'), may hold values from -6 to 6
- nominal: bfloat16 [1024, 32, 256], P('tm', 'traj'), may hold values from -6 to 6
- target: bfloat16 [1024, 32, 256], P('tm', 'traj'), may hold values from -6 to 6
- decay: float32 [1024, 256], P('tm'), may hold values from 0.4 to 1, as said below
- gain_k: bfloat16 [1024, 64, 256], P('tm'), may hold values from -0.01171875 to 0.01171875
- ctrl_b: bfloat16 [256, 64], replicated, may hold values from -0.75 to 0.75
- w_in: bfloat16 [256, 2048], replicated, may hold values from -0.375 to 0.375
- hidden_bias: float32 [2048], replicated, may hold values from -4 to 4
- w_out: bfloat16 [2048, 256], replicated, may hold values from -0.125 to 0.125
Outputs:
- states: float32 [1024, 32, 256], P('tm', 'traj')
- grad_in: float32 [256, 2048], P(None, 'traj')
- output_weight_gradient: float32 [2048, 256], P('traj')
- grad_bias: float32 [2048], P('traj')
Inputs may be any that keep to these rules, and one draw needn't show every extreme that they name: Every entry of decay is below 1.
All inputs are finite; a program needn't handle non-finite values.
Results may differ from a plain program's by a relative error of at most 0.0015.
Values sent between devices are 32-bit elements; how exact they have to be, the bound alone decides.
A program may use at most 256 MiB of HBM per device.

v0:
```python
import math

import jax
import jax.numpy as jnp
from jax import lax
from jax.sharding import PartitionSpec as P


def entering(array, axis, combine, identity, reverse):
    count, mine = (lax.axis_size(axis), lax.axis_index(axis))
    everything = jax.tree.map(lambda part: lax.all_gather(part, axis), array)
    start = jax.tree.map(
        lambda part, zero: jnp.broadcast_to(jnp.asarray(zero, part.dtype), part.shape),
        array,
        identity,
    )

    def lap(k, before):
        at = count - 1 - k if reverse else k
        reached = at > mine if reverse else at < mine
        new = combine(before, jax.tree.map(lambda part: part[at], everything))
        return jax.tree.map(lambda a, b: jnp.where(reached, a, b), new, before)

    return lax.fori_loop(0, count, lap, start)


def forward_join(earlier, later):
    first_mat, first_vec = earlier
    second_mat, second_vec = later
    joined = jnp.dot(second_mat, first_mat, precision=lax.Precision.HIGHEST)
    carried = jnp.dot(first_vec, second_mat.T, precision=lax.Precision.HIGHEST) + second_vec
    return (joined, carried)


def adjoint_join(earlier, later):
    upper_mat, upper_vec = earlier
    lower_mat, lower_vec = later
    joined = jnp.dot(upper_mat, lower_mat, precision=lax.Precision.HIGHEST)
    carried = jnp.dot(upper_vec, lower_mat, precision=lax.Precision.HIGHEST) + lower_vec
    return (joined, carried)


def shards(init_state, nominal, target, decay, gain_k, ctrl_b, w_in, hidden_bias, w_out):
    highest = lax.Precision.HIGHEST
    steps, traj_rows, width = nominal.shape
    count = lax.axis_size("tm")
    horizon = steps * count
    total_traj = traj_rows * lax.axis_size("traj")
    scale = 1.0 / math.sqrt(horizon * total_traj)
    eye = jnp.eye(width, dtype=jnp.float32)
    blank = jnp.zeros((traj_rows, width), jnp.float32)
    coupling = jnp.einsum("sc,tcr->tsr", ctrl_b, gain_k, preferred_element_type=jnp.float32)
    matrices = coupling + decay[:, None, :] * eye[None, :, :]
    ctrl_wide = ctrl_b.astype(jnp.float32)
    flat = nominal.reshape(steps * traj_rows, width)
    pre = jnp.dot(flat, w_in, preferred_element_type=jnp.float32) + hidden_bias
    hidden = jax.nn.silu(pre).astype(jnp.bfloat16)
    resid = jnp.dot(hidden, w_out, preferred_element_type=jnp.float32).reshape(
        steps, traj_rows, width
    )
    spread = jnp.sqrt(1.0 - decay * decay)
    forcing = spread[:, None, :] * resid

    def compose(carry, inputs):
        total, local = carry
        matrix, rate, gain, push = inputs
        inner = jnp.dot(gain.astype(jnp.float32), total, precision=highest)
        total = rate[:, None] * total + jnp.dot(ctrl_wide, inner, precision=highest)
        local = jnp.dot(local, matrix.T, precision=highest) + push
        return ((total, local), None)

    (seg_mat, seg_vec), _ = lax.scan(compose, (eye, blank), (matrices, decay, gain_k, forcing))
    prior_mat, prior_vec = entering((seg_mat, seg_vec), "tm", forward_join, (eye, blank), False)
    start_state = jnp.dot(init_state, prior_mat.T, precision=highest) + prior_vec

    def forward(state, inputs):
        matrix, push = inputs
        state = jnp.dot(state, matrix.T, precision=highest) + push
        return (state, state)

    _, states = lax.scan(forward, start_state, (matrices, forcing))
    errors = states - target.astype(jnp.float32)

    def backward(carried, inputs):
        matrix, miss = inputs
        lam = miss + carried
        return (jnp.dot(lam, matrix, precision=highest), lam)

    local_nu, _ = lax.scan(backward, blank, (matrices, errors), reverse=True)
    after_mat, after_vec = entering((seg_mat, local_nu), "tm", adjoint_join, (eye, blank), True)
    _, lams = lax.scan(backward, after_vec, (matrices, errors), reverse=True)
    adjoint = (spread[:, None, :] * lams).astype(jnp.bfloat16).reshape(steps * traj_rows, width)
    output_weight_gradient = (
        jnp.einsum("rh,rs->hs", hidden, adjoint, preferred_element_type=jnp.float32) * scale
    )
    dhid = jnp.einsum("rs,hs->rh", adjoint, w_out, preferred_element_type=jnp.float32)
    sig = jax.nn.sigmoid(pre)
    dpre = dhid * sig * (1.0 + pre * (1.0 - sig))
    grad_in = (
        jnp.einsum("rs,rh->sh", flat, dpre.astype(jnp.bfloat16), preferred_element_type=jnp.float32)
        * scale
    )
    grad_bias = jnp.sum(dpre, axis=0) * scale
    summed = lax.psum((grad_in, output_weight_gradient, grad_bias), "tm")
    grad_in, output_weight_gradient, grad_bias = (
        lax.psum_scatter(summed[0], "traj", scatter_dimension=1, tiled=True),
        lax.psum_scatter(summed[1], "traj", scatter_dimension=0, tiled=True),
        lax.psum_scatter(summed[2], "traj", scatter_dimension=0, tiled=True),
    )
    return (states, grad_in, output_weight_gradient, grad_bias)


def solution(mesh):
    in_specs = (
        P("traj", None),
        P("tm", "traj", None),
        P("tm", "traj", None),
        P("tm", None),
        P("tm", None, None),
        P(),
        P(),
        P(),
        P(),
    )
    out_specs = (P("tm", "traj", None), P(None, "traj"), P("traj", None), P("traj"))
    return jax.shard_map(shards, mesh=mesh, in_specs=in_specs, out_specs=out_specs, check_vma=False)
```

profile of v0, /device:TPU:0, one launch (start us, length us, event | category | flops | bytes accessed | tf_op | source)
XLA Modules:
  0.0 872.1 jit_solution(8749874240628991507)
XLA Ops:
  9.2 8.7 bitcast_add_fusion.4
  17.9 17.5 %copy.25 = f32[64,256,256]{2,1,0:T(8,128)} copy(f32[64,256,256]{1,2,0:T(8,128)} %bitcast_add_fusion.4) | data formatting | bytes 33554432
  35.4 5.6 multiply_convert_fusion
  43.0 229.0 %while.90 = (s32[]{:T(128)}, f32[256,256]{0,1:T(8,128)S(1)}, f32[16,256]{1,0:T(8,128)S(1)}, f32[64,256]{1,0:T(8,128)}, bf16[64,64,256]{2,1,0:T(8,128)(2,1)}, /*i...) while((s32[]{:T(128)}, f32[256,256]{0,1:T(8,128)S(1)}, ...), condition=%wide.region_1.2_spmd.clone, body=%wide.region_0.1_spmd.clone.sunk | while | flops 113385472 | bytes 1364595 | solution.py:72
  272.9 44.6 %all-gather.1 = f32[256,256]{1,0:T(8,128)S(1)} all-gather(f32[16,256]{1,0:T(8,128)S(1)} %get-tuple-element.504), channel_id=3, replica_groups=mesh['tm'=16,'traj'=2] {'tm'}, dimensions={0}, use_global_device_ids=true | all-gather | bytes 278528 | tf_op jit(solution)/shard_map/all_gather | solution.py:11
  317.5 40.1 %all-gather.5.cloned.1.call-done = f32[4096,256]{0,1:T(8,128)} async-done(((f32[256,256]{0,1:T(8,128)}), f32[4096,256]{0,1:T(8,128)}) %all-gather.5.cloned.1.call-update) | async-done | bytes 4194320 | tf_op jit(solution)/shard_map/all_gather | solution.py:11
  357.5 5.6 copy.26
  363.1 42.9 %while.91 = (s32[]{:T(128)}, f32[256,256]{1,0:T(8,128)S(1)}, f32[16,256]{1,0:T(8,128)S(1)}, s32[]{:T(128)}, f32[16,256,256]{2,1,0:T(8,128)}, /*index=5*/f32[16,16,256]{2,1,0:T(8,128)S(1)}, s32[]{:T(128)}, s32[]{:T(128)}) while((s32[]{:T(128)}, f32[256,256]{1,0:T(8,128)S(1)}, f32[16,256]{1,0:T(8,128)S(1)}, s32[]{:T(128)}, ...), condition=%wide.region_3.4_spmd.clone, body=%wide.region_2.3_spmd.clone.sunk | while | flops 213991424 | bytes 1936488 | solution.py:24
  364.4 1.3 convolution_select_fusion.2
  367.1 1.3 convolution_select_fusion.2
  406.5 82.8 %while.87 = (s32[]{:T(128)}, f32[16,256]{1,0:T(8,128)S(1)}, f32[64,16,256]{2,1,0:T(8,128)S(1)}, f32[64,256,256]{2,1,0:T(8,128)}, f32[64,16,256]{2,1,0:T(8,128)S(1)}, /*index=5*/s32[]{:T(128)}) while((s32[]{:T(128)}, f32[16,256]{1,0:T(8,128)S(1)}, f32[64,16,256]{2,1,0:T(8,128)S(1)}, f32[64,256,256]{2,1,0:T(8,128)}, ...), condition=%wide.region_5.6_spmd, body=%wide.region_4.5_spmd.sunk | while | flops 12587010 | bytes 361541 | solution.py:81
  489.6 76.6 %while.88 = (s32[]{:T(128)}, f32[16,256]{1,0:T(8,128)S(1)}, f32[64,16,256]{2,1,0:T(8,128)S(1)}, f32[64,256,256]{2,1,0:T(8,128)}, s32[]{:T(128)}, /*index=5*/s32[]{:T(128)}) while((s32[]{:T(128)}, f32[16,256]{1,0:T(8,128)S(1)}, f32[64,16,256]{2,1,0:T(8,128)S(1)}, f32[64,256,256]{2,1,0:T(8,128)}, s32[]{:T(128)}, /*index=5*/s32[]{:T(128)}) %tuple.204), condition=%wide.region_7.8_spmd, body=%wide.region_6.7_spmd.sunk | while | flops 12587011 | bytes 345169 | solution.py:89
  566.2 39.3 %all-gather.2 = f32[256,256]{1,0:T(8,128)S(1)} all-gather(f32[16,256]{1,0:T(8,128)S(1)} %get-tuple-element.508), channel_id=4, replica_groups=mesh['tm'=16,'traj'=2] {'tm'}, dimensions={0}, use_global_device_ids=true | all-gather | bytes 278528 | tf_op jit(solution)/shard_map/all_gather | solution.py:11
  605.5 20.0 %while.92 = (s32[]{:T(128)}, f32[16,256]{1,0:T(8,128)S(1)}, s32[]{:T(128)}, f32[16,256,256]{2,1,0:T(8,128)}, f32[16,16,256]{2,1,0:T(8,128)S(1)}, /*index=5*/s32[]{:T(128)}, s32[]{:T(128)}, s32[]{:T(128)}, s32[]{:T(128)}) while((s32[]{:T(128)}, f32[16,256]{1,0:T(8,128)S(1)}, s32[]{:T(128)}, f32[16,256,256]{2,1,0:T(8,128)}, ...), condition=%wide.region_9.10_spmd.clone, body=%wide.region_8.9_spmd.clone.sunk | while | flops 12599304 | bytes 363165 | solution.py:24
  625.7 77.8 %while.89 = (s32[]{:T(128)}, f32[16,256]{1,0:T(8,128)S(1)}, f32[64,16,256]{2,1,0:T(8,128)S(1)}, f32[64,16,256]{2,1,0:T(8,128)S(1)}, f32[64,256,256]{2,1,0:T(8,128)}, /*index=5*/s32[]{:T(128)}, s32[]{:T(128)}) while((s32[]{:T(128)}, f32[16,256]{1,0:T(8,128)S(1)}, f32[64,16,256]{2,1,0:T(8,128)S(1)}, f32[64,16,256]{2,1,0:T(8,128)S(1)}, ...), condition=%wide.region_11.12_spmd, body=%wide.region_10.11_spmd.sunk | while | flops 12591107 | bytes 394333 | solution.py:91
  703.7 4.9 convolution_multiply_fusion
  708.9 6.8 fusion.58
  715.8 2.7 fusion.52
  718.6 8.8 %reduce-scatter.3.cloned.1.call-done = f32[256,1024]{0,1:T(8,128)} async-done(((f32[256,2048]{0,1:T(8,128)}), f32[256,1024]{0,1:T(8,128)}) %reduce-scatter.3.cloned.1.call-update) | async-done | bytes 1048592 | tf_op jit(solution)/shard_map/reduce_scatter | solution.py:106
  728.7 2.5 all-reduce
  731.2 43.0 %psum.26 = f32[1024]{0:T(1024)} all-reduce(f32[1024]{0:T(1024)S(1)} %dynamic-slice.1), channel_id=1, replica_groups=mesh['tm'=16,'traj'=2] {'tm'}, use_global_device_ids=true, to_apply=%region_17.18 | all-reduce | flops 1024 | bytes 8192 | tf_op jit(solution)/shard_map/psum | solution.py:104
  774.3 86.5 %all-reduce.4.cloned.1.call-done = (f32[256,1024]{0,1:T(8,128)}, f32[1024,256]{1,0:T(8,128)}) async-done(((f32[256,1024]{0,1:T(8,128)}, f32[1024,256]{1,0:T(8,128)}), (f32[256,1024]{0,1:T(8,128)}, f32[1024,256]{1,0:T(8,128)})) %all-reduce.4.cloned.1.call-update) | async-done | bytes 2097168 | tf_op jit(solution)/shard_map/psum | solution.py:104
  860.8 2.5 copy.30
  863.3 2.3 copy.99
  (914 shorter events, 517.6 us)
Async XLA Ops:
  7.2 28.2 %copy-start = (bf16[256,2048]{1,0:T(8,128)(2,1)S(1)}, bf16[256,2048]{1,0:T(8,128)(2,1)}, u32[]{:S(2)}) copy-start(bf16[256,2048]{1,0:T(8,128)(2,1)} %param.27) | copy-start | bytes 3145732
  7.2 350.3 %all-gather.5.cloned.1.call-start = ((), (), s32[]{:S(2)}) async-start(), calls=%async_computation.2 | async-start | bytes 4456448 | tf_op jit(solution)/shard_map/all_gather | solution.py:11
  17.9 17.5 %copy-start.9 = (f32[2048]{0:T(1024)S(1)}, f32[2048]{0:T(1024)}, u32[]{:S(2)}) copy-start(f32[2048]{0:T(1024)} %param.28) | copy-start | bytes 24580
  35.4 5.7 copy-start.6
  41.1 2.0 copy-start.11
  272.1 0.7 copy-start.2
  272.8 445.8 %reduce-scatter.5.cloned.1.call-start = ((), (), s32[]{:S(2)}) async-start(), calls=%async_computation.4 | async-start | bytes 3145728 | tf_op jit(solution)/shard_map/reduce_scatter | solution.py:107
  317.4 88.6 %copy-start.5 = (f32[16,256]{1,0:T(8,128)S(1)}, f32[16,256]{1,0:T(8,128)}, u32[]{:S(2)}) copy-start(f32[16,256]{1,0:T(8,128)} %param.21) | copy-start | bytes 49156
  317.4 171.9 %copy-start.4 = (bf16[64,16,256]{2,1,0:T(8,128)(2,1)S(1)}, bf16[64,16,256]{2,1,0:T(8,128)(2,1)}, u32[]{:S(2)}) copy-start(bf16[64,16,256]{2,1,0:T(8,128)(2,1)} %param.23) | copy-start | bytes 1572868
  489.4 219.2 %copy-start.3 = (f32[64,16,256]{2,1,0:T(8,128)}, f32[64,16,256]{2,1,0:T(8,128)S(1)}, u32[]{:S(2)}) copy-start(f32[64,16,256]{2,1,0:T(8,128)S(1)} %get-tuple-element.1051) | copy-start | bytes 3145732
  703.7 5.2 copy-start.7
  708.7 18.8 %reduce-scatter.3.cloned.1.call-start = ((), (), s32[]{:S(2)}) async-start(), calls=%async_computation.3 | async-start | bytes 3145728 | tf_op jit(solution)/shard_map/reduce_scatter | solution.py:106
  708.9 6.9 copy-start.8
  715.8 11.7 %copy-start.10 = (u32[32]{0:T(128)S(1)}, u32[32]{0:T(128)}, u32[]{:S(2)}) copy-start(u32[32]{0:T(128)} %constant.180) | copy-start | bytes 388
  715.8 149.8 %copy-start.1 = (bf16[256,2048]{1,0:T(8,128)(2,1)S(1)}, bf16[256,2048]{1,0:T(8,128)(2,1)}, u32[]{:S(2)}) copy-start(bf16[256,2048]{1,0:T(8,128)(2,1)} %param.27) | copy-start | bytes 3145732
  718.5 142.2 %all-reduce.4.cloned.1.call-start = ((), (), s32[]{:S(2)}) async-start(), calls=%async_computation.5 | async-start | bytes 4194304 | tf_op jit(solution)/shard_map/psum | solution.py:104
Sparse Core Ops, SparseCore 0:
  272.9 84.5 all-gather.4
  708.8 5.4 reduce-scatter.4
  718.6 8.7 reduce-scatter.2
  732.8 127.8 all-reduce.3
where the time goes:
time: 889 us; the launch traced here: 872 us
  matrix products  496 us (56%)
  waiting for transfers between devices  135 us (15%)
  blocking collectives  129 us (15%)
  local copies, waits for them, and re-layouts  78.5 us (9%)
  loops' own time  15.7 us (2%)
  between operations  14.7 us (2%)
    dot_general x128, matrix products, backward(): return (jnp.dot(lam, matrix, precision=highest), lam)  148 us
    psum x1, waiting for transfers between devices, shards(): summed = lax.psum((grad_in, output_weight_gradient, grad_bias), 'tm')  86.5 us
    all_gather x2, blocking collectives, entering(): everything = jax.tree.map(lambda part: lax.all_gather(part, axis), array)  83.9 us
    dot_general x64, matrix products, compose(): local = jnp.dot(local, matrix.T, precision=highest) + push  78.8 us
    dot_general x64, matrix products, forward(): state = jnp.dot(state, matrix.T, precision=highest) + push  78.8 us
    dot_general x64, matrix products, compose(): inner = jnp.dot(gain.astype(jnp.float32), total, precision=highest)  66.4 us
    dynamic_slice x64, local copies, waits for them, and re-layouts, shards(): lax.scan(compose, (eye, blank), (matrices, decay, gain_k, forcing))  45.3 us
    psum x1, blocking collectives, shards(): summed = lax.psum((grad_in, output_weight_gradient, grad_bias), 'tm')  43 us
  transfers between devices with their start and end apart: 4, of which 3 were waited for; matrix products, arithmetic and copies ran while one was open for 1% of the time, Pallas kernels for 0%

commit v1 on v0

v1 whole, which is shorter than its diff:
```python
import functools
import math

import jax
import jax.numpy as jnp
from jax import lax
from jax.experimental import pallas as pl
from jax.experimental.pallas import tpu as pltpu
from jax.sharding import PartitionSpec as P

F32, BF16 = jnp.float32, jnp.bfloat16
CHUNK = 8
GROUP = 4
PIECES = 4
VMEM_LIMIT = 50 * 1024 * 1024


def split(x):
    high = x.astype(BF16)
    return high, (x - high.astype(F32)).astype(BF16)


def dot(a, b):
    return lax.dot_general(a, b, (((1,), (0,)), ((), ())), preferred_element_type=F32)


def dot_t(a, b):
    return lax.dot_general(a, b, (((1,), (1,)), ((), ())), preferred_element_type=F32)


def wide_dot(x, high, low, product=dot):
    rows = x.shape[0]
    x_high, x_low = split(x)
    both = product(jnp.concatenate([x_high, x_low], 0), high)
    return both[:rows] + both[rows:] + product(x_high, low)


def halves(u):
    high, low = split(u)
    lane = lax.broadcasted_iota(jnp.int32, u.shape, 1)
    return jnp.where(lane < u.shape[1] // 2, high.astype(F32), low.astype(F32)).astype(BF16)


def identity(width):
    return (
        lax.broadcasted_iota(jnp.int32, (width, width), 0)
        == lax.broadcasted_iota(jnp.int32, (width, width), 1)
    ).astype(F32)


def maps_kernel(gain, decay, bt2, part, before, after, seg, held):
    chunks, steps, _, width = gain.shape
    for c in range(chunks):
        held[c] = identity(width)

    def step(j, _):
        for c in range(chunks):
            x = held[c]
            high, low = split(x)
            k = gain[c, j]
            k2 = jnp.concatenate([k, k], 0)
            u = dot_t(high, k2) + dot_t(low, k2)
            held[c] = x * decay[c, j] + dot(halves(u), bt2[...])
        return 0

    lax.fori_loop(0, steps, step, 0)
    for c in range(chunks):
        part[0, c], part[1, c] = split(held[c])
    unit = identity(width).astype(BF16)
    zero = jnp.zeros((width, width), BF16)
    before[0, 0], before[1, 0] = unit, zero
    after[0, chunks - 1], after[1, chunks - 1] = unit, zero
    first, last = held[0], held[chunks - 1]
    for c in range(1, chunks):
        before[0, c], before[1, c] = split(first)
        first = wide_dot(first, part[0, c], part[1, c])
        d = chunks - 1 - c
        after[0, d], after[1, d] = split(last)
        if d > 0:
            last = wide_dot(held[d], after[0, d], after[1, d])
    seg[...] = first


def make_maps(gain, decay, bt2):
    chunks, _, _, width = gain.shape
    pair = jax.ShapeDtypeStruct((2, chunks, width, width), BF16)
    vmem = pl.BlockSpec(memory_space=pltpu.VMEM)
    return pl.pallas_call(
        maps_kernel,
        out_shape=(pair, pair, pair, jax.ShapeDtypeStruct((width, width), F32)),
        in_specs=[vmem] * 3,
        out_specs=(vmem,) * 4,
        scratch_shapes=[pltpu.VMEM((chunks, width, width), F32)],
        compiler_params=pltpu.CompilerParams(vmem_limit_bytes=VMEM_LIMIT),
        name="maps",
    )(gain, decay, bt2)


def rollout_kernel(
    count,
    init, forcing, target, decay, spread, gain, bt2, b2, part, before, after, seg,
    states, adjoint,
    segs, prods, vecs, covecs, came, gone, cocame, cogone,
    seg_send, seg_recv, vec_send, vec_recv, covec_send, covec_recv, hop,
):
    chunks, steps, rows, width = forcing.shape
    groups = count // GROUP
    me = lax.axis_index("tm")
    g, slot = me // GROUP, lax.rem(me, GROUP)
    base = g * GROUP

    barrier = pltpu.get_barrier_semaphore()

    def greet(to):
        pl.semaphore_signal(
            barrier, inc=1, device_id={"tm": to}, device_id_type=pl.DeviceIdType.MESH
        )

    for k in range(1, GROUP):
        greet(base + lax.rem(slot + k, GROUP))

    up, down = lax.rem(me + GROUP, count), lax.rem(me - GROUP + count, count)
    greet(up)
    greet(down)
    pl.semaphore_wait(barrier, GROUP + 1)

    def to_group(src, dst, send, recv):
        for k in range(1, GROUP):
            pltpu.make_async_remote_copy(
                src_ref=src, dst_ref=dst.at[slot], send_sem=send.at[k], recv_sem=recv.at[slot],
                device_id={"tm": base + lax.rem(slot + k, GROUP)},
                device_id_type=pl.DeviceIdType.MESH,
            ).start()

    def from_group(src, dst, send, recv):
        for k in range(1, GROUP):
            peer = lax.rem(slot + k, GROUP)
            copy = pltpu.make_async_remote_copy(
                src_ref=src, dst_ref=dst.at[peer], send_sem=send.at[k], recv_sem=recv.at[peer],
                device_id={"tm": base + peer}, device_id_type=pl.DeviceIdType.MESH,
            )
            copy.wait_send()
            copy.wait_recv()

    to_group(seg, segs, seg_send, seg_recv)

    def gain2(c, j):
        k = gain[c, j]
        return jnp.concatenate([k, k], 0)

    def forward(start, emit):
        def step(j, x):
            high, low = split(x)
            outs = []
            for c in range(chunks):
                z = dot_t(jnp.concatenate([high[c], low[c]], 0), gain2(c, j))
                outs.append(z[:rows] + z[rows:])
            push = dot(halves(jnp.concatenate(outs, 0)), bt2[...])
            x = x * decay[:, j] + push.reshape(x.shape) + forcing[:, j]
            if emit:
                states[:, j] = x
            return x

        return lax.fori_loop(0, steps, step, start)

    def backward(start, emit):
        def step(i, nu):
            j = steps - 1 - i
            lam = states[:, j] - target[:, j].astype(F32) + nu
            if emit:
                adjoint[:, j] = (spread[:, j] * lam).astype(BF16)
            high, low = split(lam.reshape(chunks * rows, width))
            z = dot(jnp.concatenate([high, low], 0), b2[...])
            u = halves(z[: chunks * rows] + z[chunks * rows :])
            outs = [
                dot(u[c * rows : (c + 1) * rows], gain2(c, j)).reshape(1, rows, width)
                for c in range(chunks)
            ]
            return lam * decay[:, j] + jnp.concatenate(outs, 0)

        return lax.fori_loop(0, steps, step, start)

    blank = jnp.zeros((chunks, rows, width), F32)
    one = jnp.zeros((rows, width), F32)

    ends = forward(blank, False)
    vec = ends[chunks - 1]
    for c in range(chunks - 1):
        vec = vec + wide_dot(ends[c], after[0, c], after[1, c])
    vecs[slot] = vec
    to_group(vecs.at[slot], vecs, vec_send, vec_recv)

    starts = [one]
    for c in range(chunks - 1):
        x = starts[-1]
        starts.append(ends[c] if c == 0 else wide_dot(x, part[0, c], part[1, c]) + ends[c])

    from_group(seg, segs, seg_send, seg_recv)
    segs[slot] = seg[...]
    unit = identity(width)
    ahead = unit
    for k in range(GROUP):
        ahead = jnp.where(k == slot, prods[0] if k > 0 else unit, ahead)
        if k == 0:
            prods[0] = segs[0]
        else:
            high, low = split(segs[k])
            prods[0] = wide_dot(prods[0], high, low)
    behind = unit
    prods[1] = unit
    for k in range(GROUP - 1, 0, -1):
        high, low = split(prods[1])
        prods[1] = wide_dot(segs[k], high, low)
        behind = jnp.where(k - 1 == slot, prods[1], behind)
    all_high, all_low = split(prods[0])
    ahead_high, ahead_low = split(ahead)
    behind_high, behind_low = split(behind)

    from_group(vecs.at[slot], vecs, vec_send, vec_recv)
    mine, total = one, vecs[0]
    for k in range(1, GROUP):
        mine = jnp.where(k == slot, total, mine)
        high, low = split(segs[k])
        total = wide_dot(total, high, low) + vecs[k]

    def hop_copy(src, dst, which, to):
        return pltpu.make_async_remote_copy(
            src_ref=src, dst_ref=dst, send_sem=hop.at[which, 0], recv_sem=hop.at[which, 1],
            device_id={"tm": to}, device_id_type=pl.DeviceIdType.MESH,
        )

    @pl.when(g == 0)
    def _():
        came[...] = init[...]

    @pl.when(g > 0)
    def _():
        hop_copy(gone, came, 0, up).wait_recv()

    entry = came[...]

    @pl.when(g < groups - 1)
    def _():
        gone[...] = wide_dot(entry, all_high, all_low) + total
        hop_copy(gone, came, 0, up).start()

    begin = wide_dot(entry, ahead_high, ahead_low) + mine
    starts = [
        (begin if c == 0 else wide_dot(begin, before[0, c], before[1, c]) + starts[c]).reshape(
            1, rows, width
        )
        for c in range(chunks)
    ]
    forward(jnp.concatenate(starts, 0), True)

    ends = backward(blank, False)
    vec = ends[0]
    for c in range(1, chunks):
        vec = vec + wide_dot(ends[c], before[0, c], before[1, c], dot_t)
    covecs[slot] = vec
    to_group(covecs.at[slot], covecs, covec_send, covec_recv)
    finals = [one] * chunks
    for c in range(chunks - 2, -1, -1):
        x = finals[c + 1]
        moved = ends[c + 1]
        if c < chunks - 2:
            moved = moved + wide_dot(x, part[0, c + 1], part[1, c + 1], dot_t)
        finals[c] = moved
    from_group(covecs.at[slot], covecs, covec_send, covec_recv)
    mine, total = one, covecs[GROUP - 1]
    for k in range(GROUP - 2, -1, -1):
        mine = jnp.where(k == slot, total, mine)
        high, low = split(segs[k])
        total = wide_dot(total, high, low, dot_t) + covecs[k]

    @pl.when(g == groups - 1)
    def _():
        cocame[...] = jnp.zeros_like(cocame)

    @pl.when(g < groups - 1)
    def _():
        hop_copy(cogone, cocame, 1, down).wait_recv()

    entry = cocame[...]

    @pl.when(g > 0)
    def _():
        cogone[...] = wide_dot(entry, all_high, all_low, dot_t) + total
        hop_copy(cogone, cocame, 1, down).start()

    begin = wide_dot(entry, behind_high, behind_low, dot_t) + mine
    finals = [
        (
            begin
            if c == chunks - 1
            else wide_dot(begin, after[0, c], after[1, c], dot_t) + finals[c]
        ).reshape(1, rows, width)
        for c in range(chunks)
    ]
    backward(jnp.concatenate(finals, 0), True)

    @pl.when(g < groups - 1)
    def _():
        hop_copy(gone, came, 0, up).wait_send()

    @pl.when(g > 0)
    def _():
        hop_copy(cogone, cocame, 1, down).wait_send()


def rollout(count, init, forcing, target, decay, spread, gain, bt2, b2, part, before, after, seg):
    chunks, steps, rows, width = forcing.shape
    vmem = pl.BlockSpec(memory_space=pltpu.VMEM)
    small = pltpu.VMEM((rows, width), F32)
    sems = pltpu.SemaphoreType.DMA((GROUP,))
    return pl.pallas_call(
        functools.partial(rollout_kernel, count),
        out_shape=(
            jax.ShapeDtypeStruct(forcing.shape, F32),
            jax.ShapeDtypeStruct(forcing.shape, BF16),
        ),
        in_specs=[vmem] * 12,
        out_specs=(vmem, vmem),
        scratch_shapes=[
            pltpu.VMEM((GROUP, width, width), F32),
            pltpu.VMEM((2, width, width), F32),
            pltpu.VMEM((GROUP, rows, width), F32),
            pltpu.VMEM((GROUP, rows, width), F32),
            small, small, small, small,
            sems, sems, sems, sems, sems, sems,
            pltpu.SemaphoreType.DMA((2, 2)),
        ],
        compiler_params=pltpu.CompilerParams(
            collective_id=0, has_side_effects=True, vmem_limit_bytes=VMEM_LIMIT
        ),
        name="rollout",
    )(init, forcing, target, decay, spread, gain, bt2, b2, part, before, after, seg)


def reduce_kernel(
    count, pieces,
    first, second, bias, out, bias_out,
    sib, acc, group_in, line_acc, line_in, bias_sib, bias_group, bias_line,
    sib_sems, group_sems, line_sems, spread_sems, share_sems, bias_sib_sems, bias_group_sems,
    bias_line_sems,
):
    groups = count // GROUP
    me, core = lax.axis_index("tm"), lax.axis_index("traj")
    g, slot = me // GROUP, lax.rem(me, GROUP)
    other = 1 - core
    half = first.shape[0] // 2
    piece = 2 * half // pieces
    part = piece // GROUP
    small = part // groups

    def peer(k):
        return lax.rem(slot + k, GROUP)

    def line(k):
        return lax.rem(g + k, groups)

    def at_peer(k):
        return {"tm": g * GROUP + peer(k)}

    def at_line(k):
        return {"tm": line(k) * GROUP + slot}

    barrier = pltpu.get_barrier_semaphore()
    targets = (
        [{"traj": other}]
        + [at_peer(k) for k in range(1, GROUP)]
        + [at_line(k) for k in range(1, groups)]
    )
    for to in targets:
        pl.semaphore_signal(barrier, inc=1, device_id=to, device_id_type=pl.DeviceIdType.MESH)
    pl.semaphore_wait(barrier, len(targets))

    def remote(src, dst, send, recv, to):
        return pltpu.make_async_remote_copy(
            src_ref=src, dst_ref=dst, send_sem=send, recv_sem=recv, device_id=to,
            device_id_type=pl.DeviceIdType.MESH,
        )

    def source(p, which):
        ref = first if p < pieces // 2 else second
        at = (p % (pieces // 2)) * piece
        return ref.at[pl.ds(pl.multiple_of(which * half + at, 8), piece)]

    def sib_copy(p):
        return remote(
            source(p, other), sib.at[p], sib_sems.at[0, p], sib_sems.at[1, p], {"traj": other}
        )

    def bias_sib_copy():
        return remote(
            bias.at[other], bias_sib, bias_sib_sems.at[0], bias_sib_sems.at[1], {"traj": other}
        )

    def group_copy(p, k, there):
        return remote(
            acc.at[p, pl.ds(pl.multiple_of(peer(k) * part, 8), part)], group_in.at[p, there],
            group_sems.at[0, p, k], group_sems.at[1, p, there], at_peer(k),
        )

    def line_copy(p, k, there):
        return remote(
            line_acc.at[p, pl.ds(pl.multiple_of(line(k) * small, 8), small)],
            line_in.at[p, there], line_sems.at[0, p, k], line_sems.at[1, p, there], at_line(k),
        )

    def spread_copy(p, k, there):
        at = pl.multiple_of(p * piece + slot * part + there * small, 8)
        here = pl.multiple_of(p * piece + slot * part + g * small, 8)
        return remote(
            out.at[pl.ds(here, small)], out.at[pl.ds(at, small)],
            spread_sems.at[0, p, k], spread_sems.at[1, p, there], at_line(k),
        )

    def share_copy(p, k, there):
        at = pl.multiple_of(p * piece + there * part, 8)
        here = pl.multiple_of(p * piece + slot * part, 8)
        return remote(
            out.at[pl.ds(here, part)], out.at[pl.ds(at, part)],
            share_sems.at[0, p, k], share_sems.at[1, p, there], at_peer(k),
        )

    def bias_group_copy(k, there):
        return remote(
            bias_group.at[slot], bias_group.at[there], bias_group_sems.at[0, k],
            bias_group_sems.at[1, there], at_peer(k),
        )

    def bias_line_copy(k, there):
        return remote(
            bias_line.at[g], bias_line.at[there], bias_line_sems.at[0, k],
            bias_line_sems.at[1, there], at_line(k),
        )

    for p in range(pieces):
        sib_copy(p).start()
    bias_sib_copy().start()
    for p in range(pieces):
        sib_copy(p).wait_recv()
        acc[p] = source(p, core)[...] + sib[p]
        for k in range(1, GROUP):
            group_copy(p, k, slot).start()
    bias_sib_copy().wait_recv()
    bias_group[slot] = bias[core] + bias_sib[...]
    for k in range(1, GROUP):
        bias_group_copy(k, slot).start()
    for p in range(pieces):
        total = acc[p, pl.ds(pl.multiple_of(slot * part, 8), part)]
        for k in range(1, GROUP):
            group_copy(p, k, peer(k)).wait_recv()
            total = total + group_in[p, peer(k)]
        line_acc[p] = total
        for k in range(1, groups):
            line_copy(p, k, g).start()
    for k in range(1, GROUP):
        bias_group_copy(k, peer(k)).wait_recv()
        bias_group_copy(k, slot).wait_send()
    total = bias_group[0]
    for k in range(1, GROUP):
        total = total + bias_group[k]
    bias_line[g] = total
    for k in range(1, groups):
        bias_line_copy(k, g).start()
    for p in range(pieces):
        total = line_acc[p, pl.ds(pl.multiple_of(g * small, 8), small)]
        for k in range(1, groups):
            line_copy(p, k, line(k)).wait_recv()
            total = total + line_in[p, line(k)]
        out[pl.ds(pl.multiple_of(p * piece + slot * part + g * small, 8), small)] = total
        for k in range(1, groups):
            spread_copy(p, k, g).start()
    for p in range(pieces):
        for k in range(1, groups):
            spread_copy(p, k, line(k)).wait_recv()
        for k in range(1, GROUP):
            share_copy(p, k, slot).start()
    for k in range(1, groups):
        bias_line_copy(k, line(k)).wait_recv()
    total = bias_line[0]
    for k in range(1, groups):
        total = total + bias_line[k]
    bias_out[...] = total
    for p in range(pieces):
        for k in range(1, GROUP):
            share_copy(p, k, peer(k)).wait_recv()
    bias_sib_copy().wait_send()
    for k in range(1, groups):
        bias_line_copy(k, g).wait_send()
    for p in range(pieces):
        sib_copy(p).wait_send()
        for k in range(1, GROUP):
            group_copy(p, k, slot).wait_send()
            share_copy(p, k, slot).wait_send()
        for k in range(1, groups):
            line_copy(p, k, g).wait_send()
            spread_copy(p, k, g).wait_send()


def reduce_all(count, first, second, bias):
    rows, width = first.shape
    groups = count // GROUP
    pieces = max(2, min(PIECES, rows // (GROUP * groups * 8)))
    piece = rows // pieces
    part = piece // GROUP
    small = part // groups
    vmem = pl.BlockSpec(memory_space=pltpu.VMEM)
    dma = pltpu.SemaphoreType.DMA
    tile = bias.shape[1:]
    return pl.pallas_call(
        functools.partial(reduce_kernel, count, pieces),
        out_shape=(
            jax.ShapeDtypeStruct((rows, width), F32),
            jax.ShapeDtypeStruct(tile, F32),
        ),
        in_specs=[vmem] * 3,
        out_specs=(vmem, vmem),
        scratch_shapes=[
            pltpu.VMEM((pieces, piece, width), F32),
            pltpu.VMEM((pieces, piece, width), F32),
            pltpu.VMEM((pieces, GROUP, part, width), F32),
            pltpu.VMEM((pieces, part, width), F32),
            pltpu.VMEM((pieces, groups, small, width), F32),
            pltpu.VMEM(tile, F32),
            pltpu.VMEM((GROUP,) + tile, F32),
            pltpu.VMEM((groups,) + tile, F32),
            dma((2, pieces)),
            dma((2, pieces, GROUP)),
            dma((2, pieces, groups)),
            dma((2, pieces, groups)),
            dma((2, pieces, GROUP)),
            dma((2,)),
            dma((2, GROUP)),
            dma((2, groups)),
        ],
        compiler_params=pltpu.CompilerParams(
            collective_id=1, has_side_effects=True, vmem_limit_bytes=VMEM_LIMIT
        ),
        name="reduce",
    )(first, second, bias)


def shards(init_state, nominal, target, decay, gain_k, ctrl_b, w_in, hidden_bias, w_out):
    steps, rows, width = nominal.shape
    count = lax.axis_size("tm")
    scale = 1.0 / math.sqrt(steps * count * rows * lax.axis_size("traj"))
    chunks = steps // CHUNK
    chunked = (chunks, CHUNK, rows, width)
    gain = gain_k.reshape(chunks, CHUNK, -1, width)
    rates = decay.reshape(chunks, CHUNK, 1, width)
    bt = ctrl_b.T
    bt2 = jnp.concatenate([bt, bt], 0)
    b2 = jnp.concatenate([ctrl_b, ctrl_b], 1)
    part, before, after, seg = make_maps(gain, rates, bt2)

    flat = nominal.reshape(steps * rows, width)
    pre = jnp.dot(flat, w_in, preferred_element_type=F32) + hidden_bias
    hidden = jax.nn.silu(pre).astype(BF16)
    resid = jnp.dot(hidden, w_out, preferred_element_type=F32).reshape(steps, rows, width)
    spread = jnp.sqrt(1.0 - decay * decay)
    forcing = spread[:, None, :] * resid

    states, adjoint = rollout(
        count, init_state, forcing.reshape(chunked), target.reshape(chunked), rates,
        spread.reshape(rates.shape), gain, bt2, b2, part, before, after, seg,
    )
    states = states.reshape(steps, rows, width)
    adjoint = adjoint.reshape(steps * rows, width)

    owg = jnp.einsum("rh,rs->hs", hidden, adjoint, preferred_element_type=F32) * scale
    dhid = jnp.einsum("rs,hs->rh", adjoint, w_out, preferred_element_type=F32)
    sig = jax.nn.sigmoid(pre)
    dpre = dhid * sig * (1.0 + pre * (1.0 - sig))
    grad_in = (
        jnp.einsum("rh,rs->hs", dpre.astype(BF16), flat, preferred_element_type=F32) * scale
    )
    grad_bias = jnp.sum(dpre, axis=0) * scale
    both, grad_bias = reduce_all(count, grad_in, owg, grad_bias.reshape(2, -1, 128))
    half = both.shape[0] // 2
    grad_in, owg, grad_bias = both[:half].T, both[half:], grad_bias.reshape(-1)
    return (states, grad_in, owg, grad_bias)


def solution(mesh):
    in_specs = (
        P("traj", None),
        P("tm", "traj", None),
        P("tm", "traj", None),
        P("tm", None),
        P("tm", None, None),
        P(),
        P(),
        P(),
        P(),
    )
    out_specs = (P("tm", "traj", None), P(None, "traj"), P("traj", None), P("traj"))
    return jax.shard_map(shards, mesh=mesh, in_specs=in_specs, out_specs=out_specs, check_vma=False)
```

time: 889 us -> 170 us (0.19); the launches traced: 872 us -> 169 us
  matrix products: 496 us -> 18.8 us
  Pallas kernels: 0 us -> 141 us
  waiting for transfers between devices: 135 us -> 0 us
  blocking collectives: 129 us -> 0 us
  local copies, waits for them, and re-layouts: 78.5 us -> 5.86 us
  loops' own time: 15.7 us -> 0 us
  between operations: 14.7 us -> 0.77 us
    dot_general x439 -> x5, matrix products: 496 us -> 18.8 us  [the longest x1 6.18 us: shards(): dhid = jnp.einsum('rs,hs->rh', adjoint, w_out, preferred_element_type=F32)]
    pallas_call x0 -> x3, Pallas kernels: none -> 141 us  [the longest x1 61.1 us: reduce_all(): pl.pallas_call(functools.partial(reduce_kernel, count, pieces), out_shape...]
    psum x1 -> x0, waiting for transfers between devices: 86.5 us -> none  [shards(): summed = lax.psum((grad_in, output_weight_gradient, grad_bias), 'tm')]
    all_gather x2 -> x0, blocking collectives: 83.9 us -> none  [entering(): everything = jax.tree.map(lambda part: lax.all_gather(part, axis), array)]
    dynamic_slice x64 -> x0, local copies, waits for them, and re-layouts: 45.3 us -> none  [shards(): lax.scan(compose, (eye, blank), (matrices, decay, gain_k, forcing))]
    psum x1 -> x0, blocking collectives: 43 us -> none  [shards(): summed = lax.psum((grad_in, output_weight_gradient, grad_bias), 'tm')]
    all_gather x1 -> x0, waiting for transfers between devices: 40.1 us -> none  [entering(): everything = jax.tree.map(lambda part: lax.all_gather(part, axis), array)]
    unnamed x31 -> x18, local copies, waits for them, and re-layouts: 25.2 us -> 3.78 us
  transfers between devices with their start and end apart: 4 -> 0, of which waited for: 3 -> 0; matrix products, arithmetic and copies ran while one was open for 1% -> 0% of each run, Pallas kernels for 0% -> 0%
where the time goes in v1:
time: 170 us; the launch traced here: 169 us
  Pallas kernels  141 us (83%)
  matrix products  18.8 us (11%)
  local copies, waits for them, and re-layouts  5.86 us (3%)
  other arithmetic  2.01 us (1%)
    pallas_call x1, Pallas kernels, reduce_all(): pl.pallas_call(functools.partial(reduce_kernel, count, pieces), out_shape...  61.1 us
    pallas_call x1, Pallas kernels, rollout(): pl.pallas_call(functools.partial(rollout_kernel, count), out_shape=(jax.S...  57.5 us
    pallas_call x1, Pallas kernels, make_maps(): pl.pallas_call(maps_kernel, out_shape=(pair, pair, pair, jax.ShapeDtypeSt...  22.7 us
    dot_general x1, matrix products, shards(): dhid = jnp.einsum('rs,hs->rh', adjoint, w_out, preferred_element_type=F32)  6.18 us
    dot_general x1, matrix products, shards(): pre = jnp.dot(flat, w_in, preferred_element_type=F32) + hidden_bias  6.09 us
    unnamed x18, local copies, waits for them, and re-layouts  3.78 us

profile of v1, /device:TPU:0, one launch (start us, length us, event | category | flops | bytes accessed | tf_op | source)
XLA Modules:
  0.0 168.8 jit_solution(12331503565035067996)
XLA Ops:
  0.6 0.0 copy-start
  0.6 0.9 pad_maximum_fusion.bt2
  1.5 0.9 reshape.48.decay
  2.4 0.9 copy.13
  3.3 0.1 pad_maximum_fusion.1.b2
  3.4 0.9 subtract_sqrt_fusion
  4.3 0.1 reshape.49.spread
  4.3 22.7 %maps.1 = (bf16[2,8,256,256]{3,2,1,0:T(8,128)(2,1)S(1)}, bf16[2,8,256,256]{3,2,1,0:T(8,128)(2,1)}, bf16[2,8,256,256]{3,2,1,0:T(8,128)(2,1)}, f32[256,256]{1,0:T(8,128)S(1)}) custom-call(bf16[8,8,64,256]{3,2,1,0:T(8,128)(2,1)} %bitcast.29, f32[8,8,1,256]{3,2,1,0:T(1,128)S(1)} %reshape.48.decay, bf16[128,256]{1,0:T(8,128)(2,1)S(1)} %pad_maximum_fusion.bt2), custom_call_target="tpu_custom_call" | custom-call | tf_op jit(solution)/shard_map/maps/pallas_call | solution.py:88
  27.1 6.1 %multiply_convert_fusion = (bf16[1024,2048]{1,0:T(8,128)(2,1)S(1)}, f32[1024,2048]{1,0:T(8,128)}) fusion(f32[2048]{0:T(1024)} %param.16, bf16[1024,256]{1,0:T(8,128)(2,1)} %bitcast.33, bf16[256,2048]{1,0:T(8,128)(2,1)S(1)} %copy-done), kind=kOutput, calls=%fused_computation.1 | convolution fusion | flops 1086324736 | bytes 14163968 | tf_op jit(solution)/shard_map/dot_general | solution.py:560
  33.2 0.0 copy-start.3
  33.2 1.2 fusion.8
  34.5 0.2 broadcast_multiply_fusion.forcing
  34.6 0.0 copy-done.2
  34.7 0.0 copy-start.6
  34.7 57.5 %rollout.1 = (f32[8,8,16,256]{3,2,1,0:T(8,128)S(1)}, bf16[8,8,16,256]{3,2,1,0:T(8,128)(2,1)S(1)}) custom-call(f32[16,256]{1,0:T(8,128)S(1)} %copy-done.3, f32[8,8,16,256]{3,2,1,0:T(8,128)S(1)} %broadcast_multiply_fusion.forcing, bf16[8,8,16,256]{3,2,1,0:T(8,128)(2,1)S(1)} %bitcast.25, f32[8,8,1,256]{3,2,1,0:T(1,128)S(1)} %reshape.48.decay, ...), custom_call_target="tpu_custom_call" | custom-call | tf_op jit(solution)/shard_map/rollout/pallas_call | solution.py:316
  92.2 6.2 %fusion.7 = (f32[2048]{0:T(1024)S(1)}, bf16[1024,2048]{1,0:T(8,128)(2,1)S(1)}) fusion(f32[1024,2048]{1,0:T(8,128)} %get-tuple-element.29, f32[2048]{0:T(1024)S(1)} %copy-done.6, bf16[1024,256]{1,0:T(8,128)(2,1)S(1)} %bitcast.27, bf16[2048,256]{1,0:T(8,128)(2,1)S(1)} %copy-done.4), kind=kOutput, calls=%fused_computation.15 | convolution fusion | flops 1096808448 | bytes 14172160 | tf_op jit(solution)/shard_map/rs,hs->rh/dot_general | solution.py:574
  98.4 0.0 copy-start.5
  98.4 2.6 %convolution_multiply_fusion.second = f32[2048,256]{1,0:T(8,128)} fusion(bf16[1024,2048]{1,0:T(8,128)(2,1)S(1)} %get-tuple-element.28, bf16[1024,256]{1,0:T(8,128)(2,1)S(1)} %bitcast.28), kind=kOutput, calls=%fused_computation.6 | convolution fusion | flops 1074266112 | bytes 6815744 | tf_op jit(solution)/shard_map/rh,rs->hs/dot_general | solution.py:573
  101.0 2.6 %fusion.2.first = f32[2048,256]{1,0:T(8,128)} fusion(bf16[1024,256]{1,0:T(8,128)(2,1)S(1)} %bitcast.34, bf16[1024,2048]{1,0:T(8,128)(2,1)S(1)} %get-tuple-element.31), kind=kOutput, calls=%fused_computation.5 | convolution fusion | flops 1074266112 | bytes 6815744 | tf_op jit(solution)/shard_map/rh,rs->hs/dot_general | solution.py:578
  103.7 61.1 %reduce.1 = (f32[2048,256]{1,0:T(8,128)S(1)}, f32[8,128]{1,0:T(8,128)S(1)}) custom-call(f32[2048,256]{1,0:T(8,128)} %fusion.2.first, f32[2048,256]{1,0:T(8,128)} %convolution_multiply_fusion.second, f32[2,8,128]{2,1,0:T(8,128)S(1)} %multiply_bitcast_fusion.bias), custom_call_target="tpu_custom_call" | custom-call | tf_op jit(solution)/shard_map/reduce/pallas_call | solution.py:513
  164.8 1.1 fusion.6
  165.9 1.3 copy.15
  167.2 1.0 copy.18
  168.2 0.6 copy.19
  (10 shorter events, 0.0 us)
Async XLA Ops:
  0.6 26.5 %copy-start = (bf16[256,2048]{1,0:T(8,128)(2,1)S(1)}, bf16[256,2048]{1,0:T(8,128)(2,1)}, u32[]{:S(2)}) copy-start(bf16[256,2048]{1,0:T(8,128)(2,1)} %param.15) | copy-start | bytes 3145732
  27.1 6.1 %copy-start.1 = (bf16[2,8,256,256]{3,2,1,0:T(8,128)(2,1)}, bf16[2,8,256,256]{3,2,1,0:T(8,128)(2,1)S(1)}, u32[]{:S(2)}) copy-start(bf16[2,8,256,256]{3,2,1,0:T(8,128)(2,1)S(1)} %get-tuple-element.12.part) | copy-start | bytes 6291460
  27.1 6.1 %copy-start.4 = (bf16[2048,256]{1,0:T(8,128)(2,1)S(1)}, bf16[2048,256]{1,0:T(8,128)(2,1)}, u32[]{:S(2)}) copy-start(bf16[2048,256]{1,0:T(8,128)(2,1)} %param.17) | copy-start | bytes 3145732
  33.2 1.5 copy-start.2
  33.2 1.5 copy-start.3
  34.7 57.5 %copy-start.6 = (f32[2048]{0:T(1024)S(1)}, f32[2048]{0:T(1024)}, u32[]{:S(2)}) copy-start(f32[2048]{0:T(1024)} %param.16) | copy-start | bytes 24580
  98.4 2.7 %copy-start.5 = (bf16[64,16,256]{2,1,0:T(8,128)(2,1)S(1)}, bf16[64,16,256]{2,1,0:T(8,128)(2,1)}, u32[]{:S(2)}) copy-start(bf16[64,16,256]{2,1,0:T(8,128)(2,1)} %param.10) | copy-start | bytes 1572868

commit v2 on v1

--- a/solution.py
+++ b/solution.py
@@ -11,7 +11,7 @@
 F32, BF16 = jnp.float32, jnp.bfloat16
 CHUNK = 8
 GROUP = 4
-PIECES = 4
+PIECES = 8
 VMEM_LIMIT = 50 * 1024 * 1024
 
 

time: 170 us -> 170 us (level)
  no operation moved by 1% of the time
where the time goes in v2:
time: 170 us; the launch traced here: 169 us
  Pallas kernels  142 us (84%)
  matrix products  18.8 us (11%)
  local copies, waits for them, and re-layouts  5.86 us (3%)
  other arithmetic  2.01 us (1%)
    pallas_call x1, Pallas kernels, reduce_all(): pl.pallas_call(functools.partial(reduce_kernel, count, pieces), out_shape...  61.8 us
    pallas_call x1, Pallas kernels, rollout(): pl.pallas_call(functools.partial(rollout_kernel, count), out_shape=(jax.S...  57.5 us
    pallas_call x1, Pallas kernels, make_maps(): pl.pallas_call(maps_kernel, out_shape=(pair, pair, pair, jax.ShapeDtypeSt...  22.7 us
    dot_general x1, matrix products, shards(): dhid = jnp.einsum('rs,hs->rh', adjoint, w_out, preferred_element_type=F32)  6.18 us
    dot_general x1, matrix products, shards(): pre = jnp.dot(flat, w_in, preferred_element_type=F32) + hidden_bias  6.09 us
    unnamed x18, local copies, waits for them, and re-layouts  3.78 us

profile of v2, /device:TPU:0, one launch (start us, length us, event | category | flops | bytes accessed | tf_op | source)
XLA Modules:
  0.0 169.4 jit_solution(6400144835261286539)
XLA Ops:
  0.6 0.0 copy-start
  0.6 0.9 pad_maximum_fusion.bt2
  1.5 0.9 reshape.48.decay
  2.4 0.9 copy.13
  3.3 0.1 pad_maximum_fusion.1.b2
  3.4 0.9 subtract_sqrt_fusion
  4.3 0.1 reshape.49.spread
  4.3 22.7 %maps.1 = (bf16[2,8,256,256]{3,2,1,0:T(8,128)(2,1)S(1)}, bf16[2,8,256,256]{3,2,1,0:T(8,128)(2,1)}, bf16[2,8,256,256]{3,2,1,0:T(8,128)(2,1)}, f32[256,256]{1,0:T(8,128)S(1)}) custom-call(bf16[8,8,64,256]{3,2,1,0:T(8,128)(2,1)} %bitcast.29, f32[8,8,1,256]{3,2,1,0:T(1,128)S(1)} %reshape.48.decay, bf16[128,256]{1,0:T(8,128)(2,1)S(1)} %pad_maximum_fusion.bt2), custom_call_target="tpu_custom_call" | custom-call | tf_op jit(solution)/shard_map/maps/pallas_call | solution.py:88
  27.1 6.1 %multiply_convert_fusion = (bf16[1024,2048]{1,0:T(8,128)(2,1)S(1)}, f32[1024,2048]{1,0:T(8,128)}) fusion(f32[2048]{0:T(1024)} %param.16, bf16[1024,256]{1,0:T(8,128)(2,1)} %bitcast.33, bf16[256,2048]{1,0:T(8,128)(2,1)S(1)} %copy-done), kind=kOutput, calls=%fused_computation.1 | convolution fusion | flops 1086324736 | bytes 14163968 | tf_op jit(solution)/shard_map/dot_general | solution.py:560
  33.2 0.0 copy-done.1
  33.2 0.0 copy-start.3
  33.2 1.2 fusion.8
  34.5 0.2 broadcast_multiply_fusion.forcing
  34.7 0.0 copy-start.6
  34.7 57.5 %rollout.1 = (f32[8,8,16,256]{3,2,1,0:T(8,128)S(1)}, bf16[8,8,16,256]{3,2,1,0:T(8,128)(2,1)S(1)}) custom-call(f32[16,256]{1,0:T(8,128)S(1)} %copy-done.3, f32[8,8,16,256]{3,2,1,0:T(8,128)S(1)} %broadcast_multiply_fusion.forcing, bf16[8,8,16,256]{3,2,1,0:T(8,128)(2,1)S(1)} %bitcast.25, f32[8,8,1,256]{3,2,1,0:T(1,128)S(1)} %reshape.48.decay, ...), custom_call_target="tpu_custom_call" | custom-call | tf_op jit(solution)/shard_map/rollout/pallas_call | solution.py:316
  92.2 6.2 %fusion.7 = (f32[2048]{0:T(1024)S(1)}, bf16[1024,2048]{1,0:T(8,128)(2,1)S(1)}) fusion(f32[1024,2048]{1,0:T(8,128)} %get-tuple-element.29, f32[2048]{0:T(1024)S(1)} %copy-done.6, bf16[1024,256]{1,0:T(8,128)(2,1)S(1)} %bitcast.27, bf16[2048,256]{1,0:T(8,128)(2,1)S(1)} %copy-done.4), kind=kOutput, calls=%fused_computation.15 | convolution fusion | flops 1096808448 | bytes 14172160 | tf_op jit(solution)/shard_map/rs,hs->rh/dot_general | solution.py:574
  98.4 0.0 copy-start.5
  98.4 2.6 %convolution_multiply_fusion.second = f32[2048,256]{1,0:T(8,128)} fusion(bf16[1024,2048]{1,0:T(8,128)(2,1)S(1)} %get-tuple-element.28, bf16[1024,256]{1,0:T(8,128)(2,1)S(1)} %bitcast.28), kind=kOutput, calls=%fused_computation.6 | convolution fusion | flops 1074266112 | bytes 6815744 | tf_op jit(solution)/shard_map/rh,rs->hs/dot_general | solution.py:573
  101.0 2.6 %fusion.2.first = f32[2048,256]{1,0:T(8,128)} fusion(bf16[1024,256]{1,0:T(8,128)(2,1)S(1)} %bitcast.34, bf16[1024,2048]{1,0:T(8,128)(2,1)S(1)} %get-tuple-element.31), kind=kOutput, calls=%fused_computation.5 | convolution fusion | flops 1074266112 | bytes 6815744 | tf_op jit(solution)/shard_map/rh,rs->hs/dot_general | solution.py:578
  103.7 61.8 %reduce.1 = (f32[2048,256]{1,0:T(8,128)S(1)}, f32[8,128]{1,0:T(8,128)S(1)}) custom-call(f32[2048,256]{1,0:T(8,128)} %fusion.2.first, f32[2048,256]{1,0:T(8,128)} %convolution_multiply_fusion.second, f32[2,8,128]{2,1,0:T(8,128)S(1)} %multiply_bitcast_fusion.bias), custom_call_target="tpu_custom_call" | custom-call | tf_op jit(solution)/shard_map/reduce/pallas_call | solution.py:513
  165.5 1.1 fusion.6
  166.6 1.3 copy.15
  167.9 1.0 copy.18
  168.8 0.6 copy.19
  (10 shorter events, 0.0 us)
Async XLA Ops:
  0.6 26.5 %copy-start = (bf16[256,2048]{1,0:T(8,128)(2,1)S(1)}, bf16[256,2048]{1,0:T(8,128)(2,1)}, u32[]{:S(2)}) copy-start(bf16[256,2048]{1,0:T(8,128)(2,1)} %param.15) | copy-start | bytes 3145732
  27.1 6.1 %copy-start.1 = (bf16[2,8,256,256]{3,2,1,0:T(8,128)(2,1)}, bf16[2,8,256,256]{3,2,1,0:T(8,128)(2,1)S(1)}, u32[]{:S(2)}) copy-start(bf16[2,8,256,256]{3,2,1,0:T(8,128)(2,1)S(1)} %get-tuple-element.12.part) | copy-start | bytes 6291460
  27.1 6.1 %copy-start.4 = (bf16[2048,256]{1,0:T(8,128)(2,1)S(1)}, bf16[2048,256]{1,0:T(8,128)(2,1)}, u32[]{:S(2)}) copy-start(bf16[2048,256]{1,0:T(8,128)(2,1)} %param.17) | copy-start | bytes 3145732
  33.2 1.5 copy-start.2
  33.2 1.5 copy-start.3
  34.7 57.5 %copy-start.6 = (f32[2048]{0:T(1024)S(1)}, f32[2048]{0:T(1024)}, u32[]{:S(2)}) copy-start(f32[2048]{0:T(1024)} %param.16) | copy-start | bytes 24580
  98.4 2.7 %copy-start.5 = (bf16[64,16,256]{2,1,0:T(8,128)(2,1)S(1)}, bf16[64,16,256]{2,1,0:T(8,128)(2,1)}, u32[]{:S(2)}) copy-start(bf16[64,16,256]{2,1,0:T(8,128)(2,1)} %param.10) | copy-start | bytes 1572868
